TPU v7x, 32 devices: a whole 2x2x4 slice. The times are simulated.
32 devices in a mesh: wide: 8 (over z, x), narrow: 4 (over y, core).
Axes of the slice: x: 2, y: 2, z: 4, core: 2. Of those that a mesh axis runs over, the one named last changes fastest.
Arguments:
- node: bfloat16 [256, 256, 256], P('narrow'), may hold values from -6 to 6
- right_side: bfloat16 [256, 256, 256], P('narrow'), may hold values from -16 to 16
- leg_ops: bfloat16 [3, 12, 256, 256], replicated, may hold values from -0.375 to 0.375
- op_index: int32 [32, 3], P('wide'), may hold values from 0 to 11, as said below
- offsets: int32 [32], P('wide'), may hold values from 0 to 7
Outputs:
- new_node: float32 [256, 256, 256], P('narrow')
Inputs may be any that keep to these rules, and one draw needn't show every extreme that they name: `op_index`: no two triples name the same pair of leg b and leg c operators; every operator of each leg is named by some triple.
All inputs are finite; a program needn't handle non-finite values.
Results may differ from a plain program's by a relative error of at most 0.0019.
Values may be sent and summed in bfloat16 or wider, within the bound.
A program may use at most 192 MiB of HBM per device.

v0:
```python
import math

import jax
import jax.numpy as jnp
from jax import lax
from jax.sharding import PartitionSpec as P

SECTORS = 8


def two_legs(rounded, leg_ops, op_index, triple):
    op_b = leg_ops[1, op_index[triple, 1]]
    op_c = leg_ops[2, op_index[triple, 2]]
    first = jnp.einsum("abc,qc->abq", rounded, op_c, preferred_element_type=jnp.float32).astype(
        jnp.bfloat16
    )
    return jnp.einsum("pb,abq->paq", op_b, first, preferred_element_type=jnp.float32).astype(
        jnp.bfloat16
    )


def third_leg(regrouped, leg_ops, op_index, offsets, triple, sector):
    op_a = jnp.roll(leg_ops[0, op_index[triple, 0]], offsets[triple] * sector, axis=0)
    return jnp.einsum("ra,paq->rpq", op_a, regrouped, preferred_element_type=jnp.float32)


def per_device(node, right_side, leg_ops, op_index, offsets):
    bond = node.shape[1]
    sector = bond // SECTORS
    trip_local = op_index.shape[0]
    tau = 0.5 / math.sqrt(trip_local * lax.axis_size("wide"))
    partial_value = None
    for triple in range(trip_local):
        second = two_legs(node, leg_ops, op_index, triple)
        regrouped = lax.all_to_all(second, "narrow", split_axis=0, concat_axis=1, tiled=True)
        term = third_leg(regrouped, leg_ops, op_index, offsets, triple, sector)
        partial_value = term if partial_value is None else partial_value + term
    share = lax.psum_scatter(partial_value, "wide", scatter_dimension=2, tiled=True)
    sigma = lax.all_to_all(share, "narrow", split_axis=0, concat_axis=1, tiled=True)
    width = sigma.shape[2]
    start = lax.axis_index("wide") * width
    node_cols = lax.dynamic_slice_in_dim(node, start, width, 2).astype(jnp.float32)
    right_cols = lax.dynamic_slice_in_dim(right_side, start, width, 2).astype(jnp.float32)
    updated = node_cols + tau * (right_cols - sigma)
    return lax.all_gather(updated, "wide", axis=2, tiled=True)


def solution(mesh):
    in_specs = (P("narrow", None, None), P("narrow", None, None), P(), P("wide", None), P("wide"))
    out_specs = P("narrow", None, None)
    return jax.shard_map(
        per_device, mesh=mesh, in_specs=in_specs, out_specs=out_specs, check_vma=False
    )
```

profile of v0, /device:TPU:0, one launch (start us, length us, event | category | flops | bytes accessed | tf_op | source)
XLA Modules:
  0.0 1103.0 jit_solution(13149966147575622050)
XLA Ops:
  12.2 9.0 fusion.15
  21.2 11.4 %copy.65 = bf16[256,64,256]{2,1,0:T(8,128)(2,1)} copy(bf16[256,64,256]{2,0,1:T(8,128)(2,1)} %fusion.15) | data formatting | bytes 16777216 | tf_op jit(solution)/shard_map/convert_element_type | solution.py:17
  42.3 9.0 fusion.12
  51.3 11.4 %copy.61 = bf16[256,64,256]{2,1,0:T(8,128)(2,1)} copy(bf16[256,64,256]{2,0,1:T(8,128)(2,1)} %fusion.12) | data formatting | bytes 16777216 | tf_op jit(solution)/shard_map/convert_element_type | solution.py:17
  62.7 69.5 %all-to-all-done.1 = bf16[256,64,256]{2,1,0:T(8,128)(2,1)} async-done(((bf16[256,64,256]{2,1,0:T(8,128)(2,1)}), bf16[256,64,256]{2,1,0:T(8,128)(2,1)}, u32[]{:S(2)}, u32[]{:S(2)}) %all-to-all-start.1) | async-done | bytes 8388640 | tf_op jit(solution)/shard_map/all_to_all | solution.py:35
  141.6 9.0 fusion.18
  150.6 11.4 %copy.69 = bf16[256,64,256]{2,1,0:T(8,128)(2,1)} copy(bf16[256,64,256]{2,0,1:T(8,128)(2,1)} %fusion.18) | data formatting | bytes 16777216 | tf_op jit(solution)/shard_map/convert_element_type | solution.py:17
  162.0 69.4 %all-to-all-done = bf16[256,64,256]{2,1,0:T(8,128)(2,1)} async-done(((bf16[256,64,256]{2,1,0:T(8,128)(2,1)}), bf16[256,64,256]{2,1,0:T(8,128)(2,1)}, u32[]{:S(2)}, u32[]{:S(2)}) %all-to-all-start) | async-done | bytes 8388640 | tf_op jit(solution)/shard_map/all_to_all | solution.py:35
  241.1 9.0 fusion.21
  250.1 11.4 %copy.73 = bf16[256,64,256]{2,1,0:T(8,128)(2,1)} copy(bf16[256,64,256]{2,0,1:T(8,128)(2,1)} %fusion.21) | data formatting | bytes 16777216 | tf_op jit(solution)/shard_map/convert_element_type | solution.py:17
  261.5 69.1 %all-to-all-done.2 = bf16[256,64,256]{2,1,0:T(8,128)(2,1)} async-done(((bf16[256,64,256]{2,1,0:T(8,128)(2,1)}), bf16[256,64,256]{2,1,0:T(8,128)(2,1)}, u32[]{:S(2)}, u32[]{:S(2)}) %all-to-all-start.2) | async-done | bytes 8388640 | tf_op jit(solution)/shard_map/all_to_all | solution.py:35
  348.7 8.3 copy.66
  356.9 8.3 copy.62
  365.2 8.4 copy.70
  373.6 55.9 %all-to-all-done.3 = bf16[256,64,256]{2,1,0:T(8,128)(2,1)} async-done(((bf16[256,64,256]{2,1,0:T(8,128)(2,1)}), bf16[256,64,256]{2,1,0:T(8,128)(2,1)}, u32[]{:S(2)}, u32[]{:S(2)}) %all-to-all-start.3) | async-done | bytes 8388640 | tf_op jit(solution)/shard_map/all_to_all | solution.py:35
  429.5 8.3 copy.74
  437.8 12.8 %fusion.41 = f32[256,64,256]{0,2,1:T(8,128)} fusion(bf16[64,256,256]{2,1,0:T(8,128)(2,1)} %bitcast.135, s32[]{:T(128)S(6)} %select_n.72, bf16[256,256]{1,0:T(8,128)(2,1)S(1)} %get-tuple-element.7), kind=kOutput, calls=%fused_computation.37 | convolution fusion | flops 2147745792 | bytes 25296900 | tf_op jit(solution)/shard_map/ra,paq->rpq/dot_general | solution.py:24
  450.6 12.8 %fusion.45 = f32[256,64,256]{0,2,1:T(8,128)} fusion(bf16[64,256,256]{2,1,0:T(8,128)(2,1)} %bitcast.134, s32[]{:T(128)S(6)} %select_n.70, bf16[256,256]{1,0:T(8,128)(2,1)S(1)} %get-tuple-element.9), kind=kOutput, calls=%fused_computation.40 | convolution fusion | flops 2147745792 | bytes 25296900 | tf_op jit(solution)/shard_map/ra,paq->rpq/dot_general | solution.py:24
  463.3 9.9 fusion.37
  473.2 26.5 %add_add_fusion = f32[256,64,256]{0,2,1:T(8,128)} fusion(f32[256,64,256]{0,2,1:T(8,128)} %fusion.37, f32[256,64,256]{0,2,1:T(8,128)} %fusion.45, f32[256,64,256]{0,2,1:T(8,128)} %fusion.41, bf16[64,256,256]{2,1,0:T(8,128)(2,1)} %bitcast.136, s32[]{:T(128)S(6)} %select_n.76, bf16[256,256]{1,0:T(8,128)(2,1)S(1)} %get-tuple-element.6), kind=kOutput, calls=%fused_computation | convolution fusion | flops 2160328704 | bytes 75628544 | tf_op jit(solution)/shard_map/ra,paq->rpq/dot_general | solution.py:24
  499.8 284.0 %reduce-scatter.2.cloned.1.call-done = f32[256,64,32]{0,2,1:T(8,128)} async-done(((f32[256,64,256]{0,2,1:T(8,128)}), f32[256,64,32]{0,2,1:T(8,128)}) %reduce-scatter.2.cloned.1.call-update) | async-done | bytes 2097168 | tf_op jit(solution)/shard_map/reduce_scatter | solution.py:38
  826.1 7.8 reduce
  852.2 225.8 %all-gather.2.cloned.1.call-done = f32[64,256,256]{1,0,2:T(8,128)} async-done(((f32[64,256,32]{1,0,2:T(8,128)}), f32[64,256,256]{1,0,2:T(8,128)}) %all-gather.2.cloned.1.call-update) | async-done | bytes 16777232 | tf_op jit(solution)/shard_map/all_gather | solution.py:45
  1078.0 17.6 %copy.78 = f32[64,256,256]{2,1,0:T(8,128)} copy(f32[64,256,256]{1,0,2:T(8,128)} %all-gather.2.cloned.1.call-done) | data formatting | bytes 33554432 | tf_op jit(solution)/shard_map/all_gather | solution.py:45
  (33 shorter events, 87.9 us)
Async XLA Ops:
  32.6 99.7 %all-to-all-start.1 = ((bf16[256,64,256]{2,1,0:T(8,128)(2,1)}), bf16[256,64,256]{2,1,0:T(8,128)(2,1)}, u32[]{:S(2)}, u32[]{:S(2)}) async-start(bf16[256,64,256]{2,1,0:T(8,128)(2,1)} %copy.65), calls=%async_computation.1 | async-start | bytes 16777216 | tf_op jit(solution)/shard_map/all_to_all | solution.py:35
  132.3 99.1 %all-to-all-start = ((bf16[256,64,256]{2,1,0:T(8,128)(2,1)}), bf16[256,64,256]{2,1,0:T(8,128)(2,1)}, u32[]{:S(2)}, u32[]{:S(2)}) async-start(bf16[256,64,256]{2,1,0:T(8,128)(2,1)} %copy.61), calls=%async_computation | async-start | bytes 16777216 | tf_op jit(solution)/shard_map/all_to_all | solution.py:35
  231.4 99.3 %all-to-all-start.2 = ((bf16[256,64,256]{2,1,0:T(8,128)(2,1)}), bf16[256,64,256]{2,1,0:T(8,128)(2,1)}, u32[]{:S(2)}, u32[]{:S(2)}) async-start(bf16[256,64,256]{2,1,0:T(8,128)(2,1)} %copy.69), calls=%async_computation.2 | async-start | bytes 16777216 | tf_op jit(solution)/shard_map/all_to_all | solution.py:35
  261.5 75.0 %copy-start.1 = (s32[4]{0:T(128)S(1)}, s32[4]{0:T(128)}, u32[]{:S(2)}) copy-start(s32[4]{0:T(128)} %param.11) | copy-start | bytes 52
  330.6 98.9 %all-to-all-start.3 = ((bf16[256,64,256]{2,1,0:T(8,128)(2,1)}), bf16[256,64,256]{2,1,0:T(8,128)(2,1)}, u32[]{:S(2)}, u32[]{:S(2)}) async-start(bf16[256,64,256]{2,1,0:T(8,128)(2,1)} %copy.73), calls=%async_computation.3 | async-start | bytes 16777216 | tf_op jit(solution)/shard_map/all_to_all | solution.py:35
  336.3 447.5 %reduce-scatter.2.cloned.1.call-start = ((), (), s32[]{:S(2)}) async-start(), calls=%async_computation.6 | async-start | bytes 18874368 | tf_op jit(solution)/shard_map/reduce_scatter | solution.py:38
  437.8 25.6 %slice-start = ((s8[8388608]{0:T(1024)(128)(4,1)}), s8[4194304]{0:T(1024)(128)(4,1)S(1)}, s32[]{:S(2)}) async-start(s8[8388608]{0:T(1024)(128)(4,1)} %bitcast.131), calls=%async_computation.8 | async-start | bytes 8388608
  450.6 12.8 %slice-start.1 = ((s8[8388608]{0:T(1024)(128)(4,1)}), s8[4194304]{0:T(1024)(128)(4,1)S(1)}, s32[]{:S(2)}) async-start(s8[8388608]{0:T(1024)(128)(4,1)} %bitcast.131), calls=%async_computation.9 | async-start | bytes 8388608
  794.9 29.3 %all-to-all-start.4 = ((f32[4,1,131072]{2,1,0:T(1,128)}), f32[4,1,131072]{2,1,0:T(1,128)S(1)}, u32[]{:S(2)}, u32[]{:S(2)}) async-start(f32[4,1,131072]{2,1,0:T(1,128)} %reshape.20), calls=%async_computation.5 | async-start | bytes 4194304 | tf_op jit(solution)/shard_map/all_to_all | solution.py:39
  798.5 279.5 %all-gather.2.cloned.1.call-start = ((), (), s32[]{:S(2)}) async-start(), calls=%async_computation.7 | async-start | bytes 18874368 | tf_op jit(solution)/shard_map/all_gather | solution.py:45
  824.2 1.3 copy-start
Sparse Core Ops, SparseCore 0:
  499.9 283.8 reduce-scatter.1
  852.3 225.6 all-gather.1
where the time goes:
time: 1110 us; the launch traced here: 1100 us
  waiting for transfers between devices  780 us (70%)
  local copies, waits for them, and re-layouts  148 us (13%)
  matrix products  98.1 us (9%)
  between operations  39 us (4%)
  starting transfers between devices  27.5 us (2%)
    reduce_scatter x1, waiting for transfers between devices, per_device(): lax.psum_scatter(partial_value, 'wide', scatter_dimension=2, tiled=True)  284 us
    all_to_all x4, waiting for transfers between devices, per_device(): lax.all_to_all(second, 'narrow', split_axis=0, concat_axis=1, tiled=True)  264 us
    all_gather x1, waiting for transfers between devices, per_device(): return lax.all_gather(updated, 'wide', axis=2, tiled=True)  226 us
    dot_general x4, matrix products, third_leg(): jnp.einsum('ra,paq->rpq', op_a, regrouped, preferred_element_type=jnp.flo...  62 us
    convert_element_type x4, local copies, waits for them, and re-layouts, two_legs(): jnp.einsum('pb,abq->paq', op_b, first, preferred_element_type=jnp.float32)  45.5 us
    dot_general x4, matrix products, two_legs(): jnp.einsum('pb,abq->paq', op_b, first, preferred_element_type=jnp.float32)  36.1 us
    all_to_all x4, local copies, waits for them, and re-layouts, per_device(): lax.all_to_all(second, 'narrow', split_axis=0, concat_axis=1, tiled=True)  33.3 us
    all_to_all x4, starting transfers between devices, per_device(): lax.all_to_all(second, 'narrow', split_axis=0, concat_axis=1, tiled=True)  23.6 us
  transfers between devices with their start and end apart: 7, of which 7 were waited for; matrix products, arithmetic and copies ran while one was open for 10% of the time, Pallas kernels for 0%

commit v1 on v0

v1 whole, which is shorter than its diff:
```python
import functools
import math

import jax
import jax.numpy as jnp
from jax import lax
from jax.experimental import pallas as pl
from jax.experimental.pallas import tpu as pltpu
from jax.sharding import PartitionSpec as P

SECTORS = 8
NT = (((1,), (1,)), ((), ()))


def sum_kernel(triples, parts, sector, table, first, ops_b, ops_a, out, op_a, second):
    block, rows, bond = first.shape[1:]
    group = max(1, 128 // rows)

    @pl.when(pl.program_id(0) == 0)
    def _():
        def shift(step, carry):
            pieces = []
            for place in range(group):
                triple = step * group + place
                start = pl.multiple_of(bond - table[triple, 3] * sector, sector)
                pieces.append(ops_a[table[triple, 0], pl.ds(start, bond), :])
            lanes = group * rows
            at = pl.multiple_of(step * lanes, lanes)
            op_a[:, pl.ds(at, lanes)] = jnp.concatenate(pieces, axis=1)
            return carry

        lax.fori_loop(0, triples // group, shift, 0)

    def leg_b(triple, carry):
        value = first[table[triple, 2]].reshape(block * rows, bond)
        result = lax.dot_general(
            value, ops_b[table[triple, 1]], NT, preferred_element_type=jnp.float32
        )
        at = pl.multiple_of(triple * rows, rows)
        second[:, pl.ds(at, rows), :] = result.astype(jnp.bfloat16).reshape(block, rows, bond)
        return carry

    lax.fori_loop(0, triples, leg_b, 0, unroll=4)

    def leg_a(place, carry):
        result = jnp.dot(op_a[...], second[place], preferred_element_type=jnp.float32)
        result = result.astype(jnp.bfloat16).reshape(parts, rows, bond)
        out[:, place] = result
        return carry

    lax.fori_loop(0, block, leg_a, 0)


def partial_sums(first, ops_b, ops_a, table, parts, sector):
    kops, width, rows, bond = first.shape
    triples = table.shape[0]
    block = min(width, max(1, 256 // rows))
    return pl.pallas_call(
        functools.partial(sum_kernel, triples, parts, sector),
        out_shape=jax.ShapeDtypeStruct((parts, width, rows, bond), jnp.bfloat16),
        grid_spec=pltpu.PrefetchScalarGridSpec(
            num_scalar_prefetch=1,
            grid=(width // block,),
            in_specs=[
                pl.BlockSpec((kops, block, rows, bond), lambda i, t: (0, i, 0, 0)),
                pl.BlockSpec(ops_b.shape, lambda i, t: (0, 0, 0)),
                pl.BlockSpec(ops_a.shape, lambda i, t: (0, 0, 0)),
            ],
            out_specs=pl.BlockSpec((parts, block, rows, bond), lambda i, t: (0, i, 0, 0)),
            scratch_shapes=[
                pltpu.VMEM((bond, triples * rows), jnp.bfloat16),
                pltpu.VMEM((block, triples * rows, bond), jnp.bfloat16),
            ],
        ),
        compiler_params=pltpu.CompilerParams(vmem_limit_bytes=40 * 2**20),
    )(table, first, ops_b, ops_a)


def per_device(node, right_side, leg_ops, op_index, offsets):
    rows, bond = node.shape[0], node.shape[1]
    sector = bond // SECTORS
    wide, narrow = lax.axis_size("wide"), lax.axis_size("narrow")
    triples = op_index.shape[0] * wide
    tau = 0.5 / math.sqrt(triples)
    width = bond // wide
    table = jnp.concatenate([op_index, offsets[:, None]], axis=1)
    table = lax.all_gather(table, "wide", axis=0, tiled=True)
    ops_c = lax.dynamic_slice_in_dim(leg_ops[2], lax.axis_index("wide") * width, width, 1)
    ops_a = lax.dynamic_slice_in_dim(leg_ops[0], lax.axis_index("narrow") * rows, rows, 2)
    ops_a = jnp.concatenate([ops_a, ops_a], axis=1)
    first = jnp.einsum("kqc,abc->kqab", ops_c, node, preferred_element_type=jnp.float32).astype(
        jnp.bfloat16
    )
    partial_value = partial_sums(first, leg_ops[1], ops_a, table, narrow, sector)
    share = lax.psum_scatter(partial_value, "narrow", scatter_dimension=0, tiled=False)
    sigma = lax.all_gather(share, "wide", axis=0, tiled=True)
    sigma = jnp.transpose(sigma, (1, 2, 0)).astype(jnp.float32)
    return node.astype(jnp.float32) + tau * (right_side.astype(jnp.float32) - sigma)


def solution(mesh):
    in_specs = (P("narrow", None, None), P("narrow", None, None), P(), P("wide", None), P("wide"))
    out_specs = P("narrow", None, None)
    return jax.shard_map(
        per_device, mesh=mesh, in_specs=in_specs, out_specs=out_specs, check_vma=False
    )
```

time: 1110 us -> 319 us (0.29)
  waiting for transfers between devices: 780 us -> 147 us
  matrix products: 98.1 us -> 12 us
  local copies, waits for them, and re-layouts: 148 us -> 62.4 us
  Pallas kernels: 0 us -> 40.3 us
  blocking collectives: 0 us -> 27.8 us
  starting transfers between devices: 27.5 us -> 0.04 us
  between operations: 39 us -> 13.4 us
    all_to_all x5 -> x0, waiting for transfers between devices: 270 us -> none  [the longest x4 264 us: per_device(): lax.all_to_all(second, 'narrow', split_axis=0, concat_axis=1, tiled=True)]
    reduce_scatter x1, waiting for transfers between devices: 284 us -> 44.1 us  [per_device(): lax.psum_scatter(partial_value, 'narrow', scatter_dimension=0, tiled=False)]
    all_gather x1, waiting for transfers between devices: 226 us -> 103 us  [per_device(): sigma = lax.all_gather(share, 'wide', axis=0, tiled=True)]
    dot_general x8 -> x1, matrix products: 98.1 us -> 12 us  [per_device(): jnp.einsum('kqc,abc->kqab', ops_c, node, preferred_element_type=jnp.float32)]
    convert_element_type x4 -> x0, local copies, waits for them, and re-layouts: 45.5 us -> none  [two_legs(): jnp.einsum('pb,abq->paq', op_b, first, preferred_element_type=jnp.float32)]
    all_to_all x7 -> x0, local copies, waits for them, and re-layouts: 45.1 us -> none  [the longest x4 33.3 us: per_device(): lax.all_to_all(second, 'narrow', split_axis=0, concat_axis=1, tiled=True)]
    pallas_call x0 -> x1, Pallas kernels: none -> 40.3 us  [partial_sums(): pl.pallas_call(functools.partial(sum_kernel, triples, parts, sector), out...]
    all_gather x0 -> x1, blocking collectives: none -> 27.8 us  [per_device(): table = lax.all_gather(table, 'wide', axis=0, tiled=True)]
  transfers between devices with their start and end apart: 7 -> 2, of which waited for: 7 -> 2; matrix products, arithmetic and copies ran while one was open for 10% -> 8% of each run, Pallas kernels for 0% -> 0%
where the time goes in v1:
time: 319 us; the launch traced here: 318 us
  waiting for transfers between devices  147 us (46%)
  local copies, waits for them, and re-layouts  62.4 us (20%)
  Pallas kernels  40.3 us (13%)
  blocking collectives  27.8 us (9%)
  other arithmetic  15.5 us (5%)
  between operations  13.4 us (4%)
  matrix products  12 us (4%)
    all_gather x1, waiting for transfers between devices, per_device(): sigma = lax.all_gather(share, 'wide', axis=0, tiled=True)  103 us
    reduce_scatter x1, waiting for transfers between devices, per_device(): lax.psum_scatter(partial_value, 'narrow', scatter_dimension=0, tiled=False)  44.1 us
    pallas_call x1, Pallas kernels, partial_sums(): pl.pallas_call(functools.partial(sum_kernel, triples, parts, sector), out...  40.3 us
    all_gather x1, blocking collectives, per_device(): table = lax.all_gather(table, 'wide', axis=0, tiled=True)  27.8 us
    unnamed x8, local copies, waits for them, and re-layouts  26.6 us
    add x1, local copies, waits for them, and re-layouts, per_device(): node.astype(jnp.float32) + tau * (right_side.astype(jnp.float32) - sigma)  17.6 us
    add x1, other arithmetic, per_device(): node.astype(jnp.float32) + tau * (right_side.astype(jnp.float32) - sigma)  15.1 us
    dot_general x1, local copies, waits for them, and re-layouts, per_device(): jnp.einsum('kqc,abc->kqab', ops_c, node, preferred_element_type=jnp.float32)  14 us
  transfers between devices with their start and end apart: 2, of which 2 were waited for; matrix products, arithmetic and copies ran while one was open for 8% of the time, Pallas kernels for 0%

profile of v1, /device:TPU:0, one launch (start us, length us, event | category | flops | bytes accessed | tf_op | source)
XLA Modules:
  0.0 318.2 jit_solution(40815852618613667)
XLA Ops:
  6.5 0.0 reduce-scatter.2.cloned.1.call-start
  6.5 3.9 %fusion.8 = (bf16[1,12,256,256]{3,2,1,0:T(8,128)(2,1)S(1)}, bf16[1,12,256,256]{3,2,1,0:T(8,128)(2,1)}, bf16[12,256,256]{2,1,0:T(8,128)(2,1)S(1)}) fusion(bf16[3,12,256,256]{3,2,1,0:T(8,128)(2,1)} %param.7), kind=kLoop, calls=%fused_computation.14 | loop fusion | bytes 9437184 | tf_op jit(solution)/shard_map/slice | solution.py:89
  10.4 12.0 %fusion.3 = bf16[12,32,64,256]{3,1,2,0:T(8,128)(2,1)} fusion(bf16[64,256,256]{2,1,0:T(8,128)(2,1)} %param.5, bf16[1,12,256,256]{3,2,1,0:T(8,128)(2,1)} %get-tuple-element.6, s32[]{:T(128)S(6)} %select_n.6), kind=kOutput, calls=%fused_computation.5 | convolution fusion | flops 3221225472 | bytes 21168132 | tf_op jit(solution)/shard_map/kqc,abc->kqab/dot_general | solution.py:91
  22.4 0.0 copy-start.2
  22.4 14.0 %copy.31.first = bf16[12,32,64,256]{3,2,1,0:T(8,128)(2,1)} copy(bf16[12,32,64,256]{3,1,2,0:T(8,128)(2,1)} %fusion.3) | data formatting | bytes 25165824 | tf_op jit(solution)/shard_map/kqc,abc->kqab/dot_general | solution.py:91
  36.4 0.3 dynamic-slice_bitcast_fusion
  36.6 0.4 pad_maximum_fusion.ops_a
  37.0 0.0 copy-done.2
  37.0 0.1 copy.22
  37.1 0.0 copy-done.1
  37.1 0.1 add_bitcast_fusion
  37.2 27.8 %all-gather.1 = s32[8,4,4]{2,1,0:T(4,128)S(1)} all-gather(s32[1,4,4]{2,1,0:T(4,128)S(1)} %add_bitcast_fusion), channel_id=1, replica_groups=mesh['wide'=8,'narrow'=4] {'wide'}, dimensions={0}, use_global_device_ids=true | all-gather | bytes 576 | tf_op jit(solution)/shard_map/all_gather | solution.py:87
  65.0 40.3 %shard_map.55 = bf16[4,32,64,256]{3,2,1,0:T(8,128)(2,1)S(1)} custom-call(s32[32,4]{1,0:T(8,128)S(1)} %bitcast.29, bf16[12,32,64,256]{3,2,1,0:T(8,128)(2,1)} %copy.31.first, bf16[12,256,256]{2,1,0:T(8,128)(2,1)S(1)} %get-tuple-element.7.ops_b, bf16[12,512,64]{2,1,0:T(8,128)(2,1)S(1)} %pad_maximum_fusion.ops_a), custom_call_target="tpu_custom_call" | custom-call | tf_op jit(solution)/shard_map/pallas_call | solution.py:58
  105.3 0.0 copy-start
  105.3 2.0 copy-done
  107.3 0.0 reduce-scatter.2.cloned.1.call-update
  107.3 0.0 all-gather.4.cloned.1.call-start
  107.4 44.1 %reduce-scatter.2.cloned.1.call-done = bf16[1,32,64,256]{3,2,1,0:T(8,128)(2,1)} async-done(((bf16[4,32,64,256]{3,2,1,0:T(8,128)(2,1)}), bf16[1,32,64,256]{3,2,1,0:T(8,128)(2,1)}) %reduce-scatter.2.cloned.1.call-update) | async-done | bytes 1048592 | tf_op jit(solution)/shard_map/reduce_scatter | solution.py:95
  151.4 0.0 all-gather.4.cloned.1.call-update
  151.4 12.5 %copy.20 = bf16[64,256,256]{1,0,2:T(8,128)(2,1)} copy(bf16[64,256,256]{2,1,0:T(8,128)(2,1)} %param.5) | data formatting | bytes 16777216 | tf_op args[0]
  163.9 12.1 %copy.21 = bf16[64,256,256]{1,0,2:T(8,128)(2,1)} copy(bf16[64,256,256]{2,1,0:T(8,128)(2,1)} %param.6) | data formatting | bytes 16777216 | tf_op args[1]
  176.0 102.7 %all-gather.4.cloned.1.call-done = bf16[1,256,64,256]{3,2,0,1:T(8,128)(2,1)} async-done(((bf16[1,32,64,256]{3,2,0,1:T(8,128)(2,1)}), bf16[1,256,64,256]{3,2,0,1:T(8,128)(2,1)}) %all-gather.4.cloned.1.call-update) | async-done | bytes 8388624 | tf_op jit(solution)/shard_map/all_gather | solution.py:96
  278.7 15.1 %fusion.2 = f32[64,256,256]{1,0,2:T(8,128)} fusion(bf16[64,256,256]{1,0,2:T(8,128)(2,1)} %copy.21, bf16[64,256,256]{1,0,2:T(8,128)(2,1)} %copy.20, bf16[1,256,64,256]{3,2,0,1:T(8,128)(2,1)} %all-gather.4.cloned.1.call-done), kind=kLoop, calls=%fused_computation.4 | loop fusion | flops 25165824 | bytes 41943040 | tf_op jit(solution)/shard_map/add | solution.py:98
  293.8 17.6 %copy.27 = f32[64,256,256]{2,1,0:T(8,128)} copy(f32[64,256,256]{1,0,2:T(8,128)} %fusion.2) | data formatting | bytes 33554432 | tf_op jit(solution)/shard_map/add | solution.py:98
  (1 shorter events, 0.0 us)
Async XLA Ops:
  6.5 144.9 %reduce-scatter.2.cloned.1.call-start = ((), (), s32[]{:S(2)}) async-start(), calls=%async_computation.1 | async-start | bytes 5242880 | tf_op jit(solution)/shard_map/reduce_scatter | solution.py:95
  22.4 14.6 %copy-start.2 = (s32[4]{0:T(128)S(1)}, s32[4]{0:T(128)}, u32[]{:S(2)}) copy-start(s32[4]{0:T(128)} %param.9) | copy-start | bytes 52
  22.4 14.7 %copy-start.1 = (s32[4,3]{1,0:T(4,128)S(1)}, s32[4,3]{1,0:T(4,128)}, u32[]{:S(2)}) copy-start(s32[4,3]{1,0:T(4,128)} %param.8) | copy-start | bytes 148
  105.3 2.0 copy-start
  107.3 171.4 %all-gather.4.cloned.1.call-start = ((), (), s32[]{:S(2)}) async-start(), calls=%async_computation.2 | async-start | bytes 9437184 | tf_op jit(solution)/shard_map/all_gather | solution.py:96
Sparse Core Ops, SparseCore 0:
  107.4 43.9 reduce-scatter.1
  153.7 124.9 all-gather.3

commit v2 on v1

--- a/solution.py
+++ b/solution.py
@@ -76,6 +76,33 @@
     )(table, first, ops_b, ops_a)
 
 
+def update_kernel(tau, node, right_side, sigma, out):
+    bond = node.shape[1]
+    for row in range(node.shape[0]):
+        value = sigma[:, row].reshape(bond, bond).astype(jnp.float32).T
+        right = right_side[row].astype(jnp.float32)
+        out[row] = node[row].astype(jnp.float32) + tau * (right - value)
+
+
+def update(node, right_side, sigma, tau):
+    rows, bond = node.shape[:2]
+    wide, _, width, _ = sigma.shape
+    block = min(rows, 8)
+    whole = pl.BlockSpec((block, bond, bond), lambda i: (i, 0, 0))
+    return pl.pallas_call(
+        functools.partial(update_kernel, tau),
+        out_shape=jax.ShapeDtypeStruct(node.shape, jnp.float32),
+        grid=(rows // block,),
+        in_specs=[
+            whole,
+            whole,
+            pl.BlockSpec((wide, block, width, bond), lambda i: (0, i, 0, 0)),
+        ],
+        out_specs=whole,
+        compiler_params=pltpu.CompilerParams(vmem_limit_bytes=40 * 2**20),
+    )(node, right_side, sigma)
+
+
 def per_device(node, right_side, leg_ops, op_index, offsets):
     rows, bond = node.shape[0], node.shape[1]
     sector = bond // SECTORS
@@ -84,7 +111,11 @@
     tau = 0.5 / math.sqrt(triples)
     width = bond // wide
     table = jnp.concatenate([op_index, offsets[:, None]], axis=1)
-    table = lax.all_gather(table, "wide", axis=0, tiled=True)
+    pieces = [table]
+    for step in range(1, wide):
+        ring = [(place, (place + step) % wide) for place in range(wide)]
+        pieces.append(lax.ppermute(table, "wide", ring))
+    table = jnp.concatenate(pieces, axis=0)
     ops_c = lax.dynamic_slice_in_dim(leg_ops[2], lax.axis_index("wide") * width, width, 1)
     ops_a = lax.dynamic_slice_in_dim(leg_ops[0], lax.axis_index("narrow") * rows, rows, 2)
     ops_a = jnp.concatenate([ops_a, ops_a], axis=1)
@@ -93,9 +124,9 @@
     )
     partial_value = partial_sums(first, leg_ops[1], ops_a, table, narrow, sector)
     share = lax.psum_scatter(partial_value, "narrow", scatter_dimension=0, tiled=False)
-    sigma = lax.all_gather(share, "wide", axis=0, tiled=True)
-    sigma = jnp.transpose(sigma, (1, 2, 0)).astype(jnp.float32)
-    return node.astype(jnp.float32) + tau * (right_side.astype(jnp.float32) - sigma)
+    share = jnp.swapaxes(share, 0, 1)
+    sigma = lax.all_gather(share, "wide", axis=0, tiled=True).reshape((wide,) + share.shape)
+    return update(node, right_side, sigma, tau)
 
 
 def solution(mesh):

time: 319 us -> 306 us (0.959)
  waiting for transfers between devices: 147 us -> 175 us
  blocking collectives: 27.8 us -> 0 us
  local copies, waits for them, and re-layouts: 62.4 us -> 35.8 us
  Pallas kernels: 40.3 us -> 55.3 us
  other arithmetic: 15.5 us -> 1.01 us
  starting transfers between devices: 0.04 us -> 12.6 us
    all_gather x1 -> x0, blocking collectives: 27.8 us -> none  [per_device(): table = lax.all_gather(table, 'wide', axis=0, tiled=True)]
    all_gather x1, waiting for transfers between devices: 103 us -> 127 us  [per_device(): lax.all_gather(share, 'wide', axis=0, tiled=True)]
    unnamed x8 -> x5, local copies, waits for them, and re-layouts: 26.6 us -> 6.16 us
    add x1 -> x0, local copies, waits for them, and re-layouts: 17.6 us -> none  [per_device(): node.astype(jnp.float32) + tau * (right_side.astype(jnp.float32) - sigma)]
    add x1 -> x0, other arithmetic: 15.1 us -> none  [per_device(): node.astype(jnp.float32) + tau * (right_side.astype(jnp.float32) - sigma)]
    pallas_call x0 -> x1, Pallas kernels: none -> 15 us  [update(): pl.pallas_call(functools.partial(update_kernel, tau), out_shape=jax.Shape...]
    ppermute x0 -> x7, starting transfers between devices: none -> 12.4 us  [per_device(): pieces.append(lax.ppermute(table, 'wide', ring))]
    all_gather x0 -> x1, local copies, waits for them, and re-layouts: none -> 11.4 us  [per_device(): lax.all_gather(share, 'wide', axis=0, tiled=True)]
  transfers between devices with their start and end apart: 2 -> 9, of which waited for: 2 -> 4; matrix products, arithmetic and copies ran while one was open for 8% -> 10% of each run, Pallas kernels for 0% -> 0%
where the time goes in v2:
time: 306 us
  waiting for transfers between devices  175 us (57%)
  Pallas kernels  55.3 us (18%)
  local copies, waits for them, and re-layouts  35.8 us (12%)
  between operations  13.4 us (4%)
  starting transfers between devices  12.6 us (4%)
  matrix products  12 us (4%)
    all_gather x1, waiting for transfers between devices, per_device(): lax.all_gather(share, 'wide', axis=0, tiled=True)  127 us
    reduce_scatter x1, waiting for transfers between devices, per_device(): lax.psum_scatter(partial_value, 'narrow', scatter_dimension=0, tiled=False)  42.9 us
    pallas_call x1, Pallas kernels, partial_sums(): pl.pallas_call(functools.partial(sum_kernel, triples, parts, sector), out...  40.3 us
    pallas_call x1, Pallas kernels, update(): pl.pallas_call(functools.partial(update_kernel, tau), out_shape=jax.Shape...  15 us
    dot_general x1, local copies, waits for them, and re-layouts, per_device(): jnp.einsum('kqc,abc->kqab', ops_c, node, preferred_element_type=jnp.float32)  13.9 us
    ppermute x7, starting transfers between devices, per_device(): pieces.append(lax.ppermute(table, 'wide', ring))  12.4 us
    dot_general x1, matrix products, per_device(): jnp.einsum('kqc,abc->kqab', ops_c, node, preferred_element_type=jnp.float32)  12 us
    all_gather x1, local copies, waits for them, and re-layouts, per_device(): lax.all_gather(share, 'wide', axis=0, tiled=True)  11.4 us
  transfers between devices with their start and end apart: 9, of which 4 were waited for; matrix products, arithmetic and copies ran while one was open for 10% of the time, Pallas kernels for 0%

profile of v2, /device:TPU:0, one launch (start us, length us, event | category | flops | bytes accessed | tf_op | source)
XLA Modules:
  0.0 305.6 jit_solution(2990936551018021384)
XLA Ops:
  6.5 0.8 copy.9
  7.3 0.7 pad_add_fusion
  8.0 6.0 %collective-permute-start.6 = (s32[4,4]{0,1:T(4,128)S(1)}, s32[4,4]{0,1:T(4,128)S(1)}, u32[]{:S(2)}, u32[]{:S(2)}) collective-permute-start(s32[4,4]{0,1:T(4,128)S(1)} %pad_add_fusion), channel_id=1, source_target_pairs={{0,28},{4,0},{8,4},{12,8},{16,12},{20,16},{24,20},{28,24},{1,29},{... | collective-permute-start | bytes 200 | tf_op jit(solution)/shard_map/ppermute | solution.py:117
  13.9 0.4 collective-permute-start.5
  14.4 3.0 collective-permute-start.3
  17.4 3.9 %fusion.5 = (bf16[1,12,256,256]{3,2,1,0:T(8,128)(2,1)S(1)}, bf16[1,12,256,256]{3,2,1,0:T(8,128)(2,1)}, bf16[12,256,256]{2,1,0:T(8,128)(2,1)S(1)}) fusion(bf16[3,12,256,256]{3,2,1,0:T(8,128)(2,1)} %param.7), kind=kLoop, calls=%fused_computation.10 | loop fusion | bytes 9437184 | tf_op jit(solution)/shard_map/slice | solution.py:120
  21.3 0.3 dynamic-slice_bitcast_fusion
  21.6 0.4 pad_maximum_fusion.ops_a
  21.9 12.0 %fusion = bf16[12,32,64,256]{3,1,2,0:T(8,128)(2,1)} fusion(bf16[64,256,256]{2,1,0:T(8,128)(2,1)} %node.1, bf16[1,12,256,256]{3,2,1,0:T(8,128)(2,1)} %get-tuple-element.6, s32[]{:T(128)S(6)} %select_n.6), kind=kOutput, calls=%fused_computation.1 | convolution fusion | flops 3221225472 | bytes 21168132 | tf_op jit(solution)/shard_map/kqc,abc->kqab/dot_general | solution.py:122
  33.9 13.9 %copy.15.first = bf16[12,32,64,256]{3,2,1,0:T(8,128)(2,1)} copy(bf16[12,32,64,256]{3,1,2,0:T(8,128)(2,1)} %fusion) | data formatting | bytes 25165824 | tf_op jit(solution)/shard_map/kqc,abc->kqab/dot_general | solution.py:122
  47.9 1.8 collective-permute-start.1
  49.7 1.1 collective-permute-start
  50.9 3.3 %collective-permute-done.1 = s32[4,4]{0,1:T(4,128)S(1)} collective-permute-done((s32[4,4]{0,1:T(4,128)S(1)}, s32[4,4]{0,1:T(4,128)S(1)}, u32[]{:S(2)}, u32[]{:S(2)}) %collective-permute-start.1) | collective-permute-done | bytes 96 | tf_op jit(solution)/shard_map/ppermute | solution.py:117
  54.2 1.8 collective-permute-done
  56.0 0.1 concatenate.10
  56.1 0.1 copy.11.table
  56.2 40.3 %shard_map.55 = bf16[4,32,64,256]{3,2,1,0:T(8,128)(2,1)S(1)} custom-call(s32[32,4]{1,0:T(8,128)S(1)} %copy.11.table, bf16[12,32,64,256]{3,2,1,0:T(8,128)(2,1)} %copy.15.first, bf16[12,256,256]{2,1,0:T(8,128)(2,1)S(1)} %get-tuple-element.7.ops_b, bf16[12,512,64]{2,1,0:T(8,128)(2,1)S(1)} %pad_maximum_fusion.ops_a), custom_call_target="tpu_custom_call" | custom-call | tf_op jit(solution)/shard_map/pallas_call | solution.py:58
  96.5 2.0 copy-done.1
  98.5 0.2 all-gather.2.cloned.1.call-start
  98.8 42.9 %reduce-scatter.2.cloned.1.call-done = bf16[1,32,64,256]{3,2,1,0:T(8,128)(2,1)} async-done(((bf16[4,32,64,256]{3,2,1,0:T(8,128)(2,1)}), bf16[1,32,64,256]{3,2,1,0:T(8,128)(2,1)}) %reduce-scatter.2.cloned.1.call-update) | async-done | bytes 1048592 | tf_op jit(solution)/shard_map/reduce_scatter | solution.py:126
  141.7 127.3 %all-gather.2.cloned.1.call-done = bf16[512,32,256]{2,0,1:T(8,128)(2,1)} async-done(((bf16[64,32,256]{2,0,1:T(8,128)(2,1)}), bf16[512,32,256]{2,0,1:T(8,128)(2,1)}) %all-gather.2.cloned.1.call-update) | async-done | bytes 8388624 | tf_op jit(solution)/shard_map/all_gather | solution.py:128
  269.0 11.4 %copy.12 = bf16[512,32,256]{2,1,0:T(8,128)(2,1)} copy(bf16[512,32,256]{2,0,1:T(8,128)(2,1)} %all-gather.2.cloned.1.call-done) | data formatting | bytes 16777216 | tf_op jit(solution)/shard_map/all_gather | solution.py:128
  280.4 3.4 %copy-done = bf16[64,256,256]{2,1,0:T(8,128)(2,1)S(1)} copy-done((bf16[64,256,256]{2,1,0:T(8,128)(2,1)S(1)}, bf16[64,256,256]{2,1,0:T(8,128)(2,1)}, u32[]{:S(2)}) %copy-start) | copy-done | bytes 8388632
  283.8 15.0 %shard_map.56 = f32[64,256,256]{2,1,0:T(8,128)} custom-call(bf16[64,256,256]{2,1,0:T(8,128)(2,1)S(1)} %copy-done, bf16[64,256,256]{2,1,0:T(8,128)(2,1)} %right_side.1, bf16[8,64,32,256]{3,2,1,0:T(8,128)(2,1)} %bitcast.18), custom_call_target="tpu_custom_call" | custom-call | tf_op jit(solution)/shard_map/pallas_call | solution.py:92
  (12 shorter events, 0.1 us)
Async XLA Ops:
  6.5 135.1 %reduce-scatter.2.cloned.1.call-start = ((), (), s32[]{:S(2)}) async-start(), calls=%async_computation.1 | async-start | bytes 5242880 | tf_op jit(solution)/shard_map/reduce_scatter | solution.py:126
  8.0 39.9 %collective-permute-start.6 = (s32[4,4]{0,1:T(4,128)S(1)}, s32[4,4]{0,1:T(4,128)S(1)}, u32[]{:S(2)}, u32[]{:S(2)}) collective-permute-start(s32[4,4]{0,1:T(4,128)S(1)} %pad_add_fusion), channel_id=1, source_target_pairs={{0,28},{4,0},{8,4},{12,8},{16,12},{20,16},{24,20},{28,24},{1,29},{... | collective-permute-start | bytes 200 | tf_op jit(solution)/shard_map/ppermute | solution.py:117
  13.9 35.8 %collective-permute-start.5 = (s32[4,4]{0,1:T(4,128)S(1)}, s32[4,4]{0,1:T(4,128)S(1)}, u32[]{:S(2)}, u32[]{:S(2)}) collective-permute-start(s32[4,4]{0,1:T(4,128)S(1)} %pad_add_fusion), channel_id=1, source_target_pairs={{0,24},{4,28},{8,0},{12,4},{16,8},{20,12},{24,16},{28,20},{1,25},{... | collective-permute-start | bytes 200 | tf_op jit(solution)/shard_map/ppermute | solution.py:117
  14.4 36.4 %collective-permute-start.4 = (s32[4,4]{0,1:T(4,128)S(1)}, s32[4,4]{0,1:T(4,128)S(1)}, u32[]{:S(2)}, u32[]{:S(2)}) collective-permute-start(s32[4,4]{0,1:T(4,128)S(1)} %pad_add_fusion), channel_id=1, source_target_pairs={{0,20},{4,24},{8,28},{12,0},{16,4},{20,8},{24,12},{28,16},{1,21},{... | collective-permute-start | bytes 200 | tf_op jit(solution)/shard_map/ppermute | solution.py:117
  14.4 36.4 %collective-permute-start.3 = (s32[4,4]{0,1:T(4,128)S(1)}, s32[4,4]{0,1:T(4,128)S(1)}, u32[]{:S(2)}, u32[]{:S(2)}) collective-permute-start(s32[4,4]{0,1:T(4,128)S(1)} %pad_add_fusion), channel_id=1, source_target_pairs={{0,16},{4,20},{8,24},{12,28},{16,0},{20,4},{24,8},{28,12},{1,17},{... | collective-permute-start | bytes 200 | tf_op jit(solution)/shard_map/ppermute | solution.py:117
  17.4 33.4 %collective-permute-start.2 = (s32[4,4]{0,1:T(4,128)S(1)}, s32[4,4]{0,1:T(4,128)S(1)}, u32[]{:S(2)}, u32[]{:S(2)}) collective-permute-start(s32[4,4]{0,1:T(4,128)S(1)} %pad_add_fusion), channel_id=1, source_target_pairs={{0,12},{4,16},{8,20},{12,24},{16,28},{20,0},{24,4},{28,8},{1,13},{... | collective-permute-start | bytes 200 | tf_op jit(solution)/shard_map/ppermute | solution.py:117
  47.9 6.3 %collective-permute-start.1 = (s32[4,4]{0,1:T(4,128)S(1)}, s32[4,4]{0,1:T(4,128)S(1)}, u32[]{:S(2)}, u32[]{:S(2)}) collective-permute-start(s32[4,4]{0,1:T(4,128)S(1)} %pad_add_fusion), channel_id=1, source_target_pairs={{0,8},{4,12},{8,16},{12,20},{16,24},{20,28},{24,0},{28,4},{1,9},{5... | collective-permute-start | bytes 200 | tf_op jit(solution)/shard_map/ppermute | solution.py:117
  49.7 6.3 %collective-permute-start = (s32[4,4]{0,1:T(4,128)S(1)}, s32[4,4]{0,1:T(4,128)S(1)}, u32[]{:S(2)}, u32[]{:S(2)}) collective-permute-start(s32[4,4]{0,1:T(4,128)S(1)} %pad_add_fusion), channel_id=1, source_target_pairs={{0,4},{4,8},{8,12},{12,16},{16,20},{20,24},{24,28},{28,0},{1,5},{5... | collective-permute-start | bytes 200 | tf_op jit(solution)/shard_map/ppermute | solution.py:117
  96.5 2.0 copy-start.1
  98.5 170.5 %all-gather.2.cloned.1.call-start = ((), (), s32[]{:S(2)}) async-start(), calls=%async_computation.2 | async-start | bytes 9437184 | tf_op jit(solution)/shard_map/all_gather | solution.py:128
  280.4 3.4 %copy-start = (bf16[64,256,256]{2,1,0:T(8,128)(2,1)S(1)}, bf16[64,256,256]{2,1,0:T(8,128)(2,1)}, u32[]{:S(2)}) copy-start(bf16[64,256,256]{2,1,0:T(8,128)(2,1)} %node.1) | copy-start | bytes 25165828
Sparse Core Ops, SparseCore 0:
  98.7 42.9 reduce-scatter.1
  144.0 124.8 all-gather.1

commit v3 on v2

--- a/solution.py
+++ b/solution.py
@@ -76,6 +76,19 @@
     )(table, first, ops_b, ops_a)
 
 
+def swap_kernel(value, out):
+    out[...] = jnp.swapaxes(value[...].astype(jnp.float32), 0, 1).astype(out.dtype)
+
+
+def swap_leading(value):
+    width, rows, bond = value.shape
+    return pl.pallas_call(
+        swap_kernel,
+        out_shape=jax.ShapeDtypeStruct((rows, width, bond), value.dtype),
+        compiler_params=pltpu.CompilerParams(vmem_limit_bytes=24 * 2**20),
+    )(value)
+
+
 def update_kernel(tau, node, right_side, sigma, out):
     bond = node.shape[1]
     for row in range(node.shape[0]):
@@ -124,7 +137,7 @@
     )
     partial_value = partial_sums(first, leg_ops[1], ops_a, table, narrow, sector)
     share = lax.psum_scatter(partial_value, "narrow", scatter_dimension=0, tiled=False)
-    share = jnp.swapaxes(share, 0, 1)
+    share = swap_leading(share)
     sigma = lax.all_gather(share, "wide", axis=0, tiled=True).reshape((wide,) + share.shape)
     return update(node, right_side, sigma, tau)
 

time: 306 us -> 295 us (0.964)
  local copies, waits for them, and re-layouts: 35.8 us -> 25.7 us
    all_gather x1 -> x0, local copies, waits for them, and re-layouts: 11.4 us -> none  [per_device(): lax.all_gather(share, 'wide', axis=0, tiled=True)]
    unnamed x5 -> x7, local copies, waits for them, and re-layouts: 6.16 us -> 7.38 us
where the time goes in v3:
time: 295 us
  waiting for transfers between devices  173 us (59%)
  Pallas kernels  56.7 us (19%)
  local copies, waits for them, and re-layouts  25.7 us (9%)
  between operations  13.4 us (5%)
  starting transfers between devices  12.4 us (4%)
  matrix products  12 us (4%)
    all_gather x1, waiting for transfers between devices, per_device(): lax.all_gather(share, 'wide', axis=0, tiled=True)  125 us
    reduce_scatter x1, waiting for transfers between devices, per_device(): lax.psum_scatter(partial_value, 'narrow', scatter_dimension=0, tiled=False)  43 us
    pallas_call x1, Pallas kernels, partial_sums(): pl.pallas_call(functools.partial(sum_kernel, triples, parts, sector), out...  40.3 us
    pallas_call x1, Pallas kernels, update(): pl.pallas_call(functools.partial(update_kernel, tau), out_shape=jax.Shape...  15 us
    dot_general x1, local copies, waits for them, and re-layouts, per_device(): jnp.einsum('kqc,abc->kqab', ops_c, node, preferred_element_type=jnp.float32)  13.9 us
    ppermute x7, starting transfers between devices, per_device(): pieces.append(lax.ppermute(table, 'wide', ring))  12.4 us
    dot_general x1, matrix products, per_device(): jnp.einsum('kqc,abc->kqab', ops_c, node, preferred_element_type=jnp.float32)  12 us
    unnamed x7, local copies, waits for them, and re-layouts  7.38 us
  transfers between devices with their start and end apart: 9, of which 4 were waited for; matrix products, arithmetic and copies ran while one was open for 10% of the time, Pallas kernels for 0%

profile of v3, /device:TPU:0, one launch (start us, length us, event | category | flops | bytes accessed | tf_op | source)
XLA Modules:
  0.0 294.6 jit_solution(6194095591863940183)
XLA Ops:
  6.5 0.8 copy.8
  7.3 0.7 pad_add_fusion
  8.0 6.0 %collective-permute-start.6 = (s32[4,4]{0,1:T(4,128)S(1)}, s32[4,4]{0,1:T(4,128)S(1)}, u32[]{:S(2)}, u32[]{:S(2)}) collective-permute-start(s32[4,4]{0,1:T(4,128)S(1)} %pad_add_fusion), channel_id=1, source_target_pairs={{0,28},{4,0},{8,4},{12,8},{16,12},{20,16},{24,20},{28,24},{1,29},{... | collective-permute-start | bytes 200 | tf_op jit(solution)/shard_map/ppermute | solution.py:130
  13.9 0.4 collective-permute-start.5
  14.4 3.0 %collective-permute-start.3 = (s32[4,4]{0,1:T(4,128)S(1)}, s32[4,4]{0,1:T(4,128)S(1)}, u32[]{:S(2)}, u32[]{:S(2)}) collective-permute-start(s32[4,4]{0,1:T(4,128)S(1)} %pad_add_fusion), channel_id=1, source_target_pairs={{0,16},{4,20},{8,24},{12,28},{16,0},{20,4},{24,8},{28,12},{1,17},{... | collective-permute-start | bytes 200 | tf_op jit(solution)/shard_map/ppermute | solution.py:130
  17.4 3.9 %fusion.5 = (bf16[1,12,256,256]{3,2,1,0:T(8,128)(2,1)S(1)}, bf16[1,12,256,256]{3,2,1,0:T(8,128)(2,1)}, bf16[12,256,256]{2,1,0:T(8,128)(2,1)S(1)}) fusion(bf16[3,12,256,256]{3,2,1,0:T(8,128)(2,1)} %param.7), kind=kLoop, calls=%fused_computation.10 | loop fusion | bytes 9437184 | tf_op jit(solution)/shard_map/slice | solution.py:133
  21.3 0.3 dynamic-slice_bitcast_fusion
  21.6 0.4 pad_maximum_fusion.ops_a
  22.0 12.0 %fusion = bf16[12,32,64,256]{3,1,2,0:T(8,128)(2,1)} fusion(bf16[64,256,256]{2,1,0:T(8,128)(2,1)} %node.1, bf16[1,12,256,256]{3,2,1,0:T(8,128)(2,1)} %get-tuple-element.6, s32[]{:T(128)S(6)} %select_n.6), kind=kOutput, calls=%fused_computation.1 | convolution fusion | flops 3221225472 | bytes 21168132 | tf_op jit(solution)/shard_map/kqc,abc->kqab/dot_general | solution.py:135
  33.9 13.9 %copy.13.first = bf16[12,32,64,256]{3,2,1,0:T(8,128)(2,1)} copy(bf16[12,32,64,256]{3,1,2,0:T(8,128)(2,1)} %fusion) | data formatting | bytes 25165824 | tf_op jit(solution)/shard_map/kqc,abc->kqab/dot_general | solution.py:135
  47.9 1.8 collective-permute-start.1
  49.7 1.1 collective-permute-start
  50.9 3.3 %collective-permute-done.1 = s32[4,4]{0,1:T(4,128)S(1)} collective-permute-done((s32[4,4]{0,1:T(4,128)S(1)}, s32[4,4]{0,1:T(4,128)S(1)}, u32[]{:S(2)}, u32[]{:S(2)}) %collective-permute-start.1) | collective-permute-done | bytes 96 | tf_op jit(solution)/shard_map/ppermute | solution.py:130
  54.2 1.8 collective-permute-done
  56.0 0.1 concatenate.10
  56.1 0.1 copy.10.table
  56.2 40.3 %shard_map.55 = bf16[4,32,64,256]{3,2,1,0:T(8,128)(2,1)S(1)} custom-call(s32[32,4]{1,0:T(8,128)S(1)} %copy.10.table, bf16[12,32,64,256]{3,2,1,0:T(8,128)(2,1)} %copy.13.first, bf16[12,256,256]{2,1,0:T(8,128)(2,1)S(1)} %get-tuple-element.7.ops_b, bf16[12,512,64]{2,1,0:T(8,128)(2,1)S(1)} %pad_maximum_fusion.ops_a), custom_call_target="tpu_custom_call" | custom-call | tf_op jit(solution)/shard_map/pallas_call | solution.py:58
  96.5 2.0 copy-done.1
  98.6 43.0 %reduce-scatter.2.cloned.1.call-done = bf16[1,32,64,256]{3,2,1,0:T(8,128)(2,1)} async-done(((bf16[4,32,64,256]{3,2,1,0:T(8,128)(2,1)}), bf16[1,32,64,256]{3,2,1,0:T(8,128)(2,1)}) %reduce-scatter.2.cloned.1.call-update) | async-done | bytes 1048592 | tf_op jit(solution)/shard_map/reduce_scatter | solution.py:139
  141.6 1.2 copy-done.2
  142.9 1.5 shard_map.56
  144.4 125.1 %all-gather.2.cloned.1.call-done = bf16[512,32,256]{2,1,0:T(8,128)(2,1)} async-done(((bf16[64,32,256]{2,1,0:T(8,128)(2,1)}), bf16[512,32,256]{2,1,0:T(8,128)(2,1)}) %all-gather.2.cloned.1.call-update) | async-done | bytes 8388624 | tf_op jit(solution)/shard_map/all_gather | solution.py:141
  269.4 3.4 %copy-done = bf16[64,256,256]{2,1,0:T(8,128)(2,1)S(1)} copy-done((bf16[64,256,256]{2,1,0:T(8,128)(2,1)S(1)}, bf16[64,256,256]{2,1,0:T(8,128)(2,1)}, u32[]{:S(2)}) %copy-start) | copy-done | bytes 8388632
  272.8 15.0 %shard_map.57 = f32[64,256,256]{2,1,0:T(8,128)} custom-call(bf16[64,256,256]{2,1,0:T(8,128)(2,1)S(1)} %copy-done, bf16[64,256,256]{2,1,0:T(8,128)(2,1)} %right_side.1, bf16[8,64,32,256]{3,2,1,0:T(8,128)(2,1)} %bitcast.17), custom_call_target="tpu_custom_call" | custom-call | tf_op jit(solution)/shard_map/pallas_call | solution.py:105
  (14 shorter events, 0.1 us)
Async XLA Ops:
  6.5 135.1 %reduce-scatter.2.cloned.1.call-start = ((), (), s32[]{:S(2)}) async-start(), calls=%async_computation.1 | async-start | bytes 5242880 | tf_op jit(solution)/shard_map/reduce_scatter | solution.py:139
  8.0 39.9 %collective-permute-start.6 = (s32[4,4]{0,1:T(4,128)S(1)}, s32[4,4]{0,1:T(4,128)S(1)}, u32[]{:S(2)}, u32[]{:S(2)}) collective-permute-start(s32[4,4]{0,1:T(4,128)S(1)} %pad_add_fusion), channel_id=1, source_target_pairs={{0,28},{4,0},{8,4},{12,8},{16,12},{20,16},{24,20},{28,24},{1,29},{... | collective-permute-start | bytes 200 | tf_op jit(solution)/shard_map/ppermute | solution.py:130
  13.9 35.8 %collective-permute-start.5 = (s32[4,4]{0,1:T(4,128)S(1)}, s32[4,4]{0,1:T(4,128)S(1)}, u32[]{:S(2)}, u32[]{:S(2)}) collective-permute-start(s32[4,4]{0,1:T(4,128)S(1)} %pad_add_fusion), channel_id=1, source_target_pairs={{0,24},{4,28},{8,0},{12,4},{16,8},{20,12},{24,16},{28,20},{1,25},{... | collective-permute-start | bytes 200 | tf_op jit(solution)/shard_map/ppermute | solution.py:130
  14.4 36.5 %collective-permute-start.4 = (s32[4,4]{0,1:T(4,128)S(1)}, s32[4,4]{0,1:T(4,128)S(1)}, u32[]{:S(2)}, u32[]{:S(2)}) collective-permute-start(s32[4,4]{0,1:T(4,128)S(1)} %pad_add_fusion), channel_id=1, source_target_pairs={{0,20},{4,24},{8,28},{12,0},{16,4},{20,8},{24,12},{28,16},{1,21},{... | collective-permute-start | bytes 200 | tf_op jit(solution)/shard_map/ppermute | solution.py:130
  14.4 36.5 %collective-permute-start.3 = (s32[4,4]{0,1:T(4,128)S(1)}, s32[4,4]{0,1:T(4,128)S(1)}, u32[]{:S(2)}, u32[]{:S(2)}) collective-permute-start(s32[4,4]{0,1:T(4,128)S(1)} %pad_add_fusion), channel_id=1, source_target_pairs={{0,16},{4,20},{8,24},{12,28},{16,0},{20,4},{24,8},{28,12},{1,17},{... | collective-permute-start | bytes 200 | tf_op jit(solution)/shard_map/ppermute | solution.py:130
  17.4 33.4 %collective-permute-start.2 = (s32[4,4]{0,1:T(4,128)S(1)}, s32[4,4]{0,1:T(4,128)S(1)}, u32[]{:S(2)}, u32[]{:S(2)}) collective-permute-start(s32[4,4]{0,1:T(4,128)S(1)} %pad_add_fusion), channel_id=1, source_target_pairs={{0,12},{4,16},{8,20},{12,24},{16,28},{20,0},{24,4},{28,8},{1,13},{... | collective-permute-start | bytes 200 | tf_op jit(solution)/shard_map/ppermute | solution.py:130
  47.9 6.3 %collective-permute-start.1 = (s32[4,4]{0,1:T(4,128)S(1)}, s32[4,4]{0,1:T(4,128)S(1)}, u32[]{:S(2)}, u32[]{:S(2)}) collective-permute-start(s32[4,4]{0,1:T(4,128)S(1)} %pad_add_fusion), channel_id=1, source_target_pairs={{0,8},{4,12},{8,16},{12,20},{16,24},{20,28},{24,0},{28,4},{1,9},{5... | collective-permute-start | bytes 200 | tf_op jit(solution)/shard_map/ppermute | solution.py:130
  49.7 6.3 %collective-permute-start = (s32[4,4]{0,1:T(4,128)S(1)}, s32[4,4]{0,1:T(4,128)S(1)}, u32[]{:S(2)}, u32[]{:S(2)}) collective-permute-start(s32[4,4]{0,1:T(4,128)S(1)} %pad_add_fusion), channel_id=1, source_target_pairs={{0,4},{4,8},{8,12},{12,16},{16,20},{20,24},{24,28},{28,0},{1,5},{5... | collective-permute-start | bytes 200 | tf_op jit(solution)/shard_map/ppermute | solution.py:130
  96.5 2.0 copy-start.1
  98.5 170.9 %all-gather.2.cloned.1.call-start = ((), (), s32[]{:S(2)}) async-start(), calls=%async_computation.2 | async-start | bytes 9437184 | tf_op jit(solution)/shard_map/all_gather | solution.py:141
  141.6 1.2 copy-start.2
  269.4 3.4 %copy-start = (bf16[64,256,256]{2,1,0:T(8,128)(2,1)S(1)}, bf16[64,256,256]{2,1,0:T(8,128)(2,1)}, u32[]{:S(2)}) copy-start(bf16[64,256,256]{2,1,0:T(8,128)(2,1)} %node.1) | copy-start | bytes 25165828
Sparse Core Ops, SparseCore 0:
  98.7 42.9 reduce-scatter.1
  144.5 124.8 all-gather.1
